TPU v7x, 32 devices: a whole 2x2x4 slice. The times are simulated.
32 devices in a mesh: groups: 2 (over y), dp: 4 (over x, core), mp: 4 (over z).
Axes of the slice: x: 2, y: 2, z: 4, core: 2. Of those that a mesh axis runs over, the one named last changes fastest.
Arguments:
- attn_out: bfloat16 [4096, 8192], P(('groups', 'dp'), 'mp'), parts along dimension 0, may hold values from -6 to 6
- out_weight: bfloat16 [8192, 8192], P(None, 'mp'), may hold values from -0.0625 to 0.0625
- cotangent: bfloat16 [4096, 8192], P(('groups', 'dp'), 'mp'), parts along dimension 0, may hold values from -6 to 6
- proj_in_w: bfloat16 [8192, 64], replicated, may hold values from -0.0625 to 0.0625
- proj_out_w: bfloat16 [8192, 64], replicated, may hold values from -0.0625 to 0.0625
- queries: bfloat16 [1024, 4096], P('mp', 'dp'), may hold values from -0.005859375 to 0.005859375
- lengths: int32 [16], P(('groups', 'dp')), parts along dimension 0, may hold values from 1 to 256, 1536 in all
Outputs:
- layer_out: bfloat16 [4096, 8192], P(('groups', 'dp'), 'mp'), parts along dimension 0
- grad_in: bfloat16 [4096, 8192], P(('groups', 'dp'), 'mp'), parts along dimension 0
- scores: float32 [16, 1024], P(('groups', 'dp'), 'mp'), parts along dimension 0
There are 2 independent parts, one for each index of `groups`. A program takes and returns all parts, laid end to end along the dimension named above; an argument that names none is the same for every part. Nothing has to cross between parts.
Inputs may be any that keep to these rules, and one draw needn't show every extreme that they name: Live tokens sit at the start of a sequence; some sequence of each part has exactly 256; the lengths of one part sum to 1536.
All inputs are finite; a program needn't handle non-finite values. No bound on the sum of `lengths` on one device may be relied on, other than what follows from the above.
Results may differ from a plain program's by a relative error of at most 0.001.
Values may be sent and summed in bfloat16 or wider, within the bound.
A program may use at most 192 MiB of HBM per device.

v0:
```python
import jax
import jax.numpy as jnp
from jax import lax
from jax.sharding import PartitionSpec as P

LEN = 256


HIGHEST_PRECISION = lax.Precision.HIGHEST


def per_device(attn_out, out_weight, cotangent, proj_in_w, proj_out_w, queries, lengths):
    tok_rows = attn_out.shape[0]
    block_width = attn_out.shape[1]
    rank_width = proj_in_w.shape[1]
    seq_count = lengths.shape[0]
    block_start = lax.axis_index("mp") * block_width
    local_in_w = lax.dynamic_slice_in_dim(proj_in_w, block_start, block_width, 0)
    local_out_w = lax.dynamic_slice_in_dim(proj_out_w, block_start, block_width, 0)
    forward = jnp.dot(
        lax.all_gather(attn_out, "mp", axis=1, tiled=True),
        out_weight,
        preferred_element_type=jnp.float32,
    )
    part_in = jnp.dot(attn_out, local_in_w, preferred_element_type=jnp.float32)
    part_out = jnp.dot(cotangent, local_out_w, preferred_element_type=jnp.float32)
    proj_in, proj_out = lax.psum((part_in, part_out), "mp")
    layer_out = forward.astype(jnp.bfloat16)
    grad_term_full = lax.dot_general(
        cotangent, out_weight, (((1,), (1,)), ((), ())), preferred_element_type=jnp.float32
    )
    grad_in = lax.psum_scatter(grad_term_full, "mp", scatter_dimension=1, tiled=True).astype(
        jnp.bfloat16
    )
    slot_index = jnp.arange(tok_rows, dtype=jnp.int32)
    example_ids = slot_index // LEN
    offsets = slot_index % LEN
    seq_slots = jnp.arange(seq_count, dtype=jnp.int32)
    live_table = (example_ids[:, None] == seq_slots[None, :]) & (
        offsets[:, None] < lengths[None, :]
    )
    live_rows = jnp.sum(live_table.astype(jnp.float32), axis=1)
    weighted = (proj_in * live_rows[:, None]).reshape(seq_count, LEN, rank_width)
    kronecker = jnp.einsum(
        "eti,etj->eij",
        weighted,
        proj_out.reshape(seq_count, LEN, rank_width),
        precision=HIGHEST_PRECISION,
    ).reshape(seq_count, rank_width * rank_width)
    scores = lax.dot_general(
        kronecker,
        lax.all_gather(queries, "dp", axis=1, tiled=True).astype(jnp.float32),
        (((1,), (1,)), ((), ())),
        precision=HIGHEST_PRECISION,
        preferred_element_type=jnp.float32,
    )
    return (layer_out, grad_in, scores)


def solution(mesh):
    in_specs = (
        P(("groups", "dp"), "mp"),
        P(None, "mp"),
        P(("groups", "dp"), "mp"),
        P(),
        P(),
        P("mp", "dp"),
        P(("groups", "dp")),
    )
    out_specs = (P(("groups", "dp"), "mp"), P(("groups", "dp"), "mp"), P(("groups", "dp"), "mp"))
    return jax.shard_map(
        per_device, mesh=mesh, in_specs=in_specs, out_specs=out_specs, check_vma=False
    )
```

profile of v0, /device:TPU:0, one launch (start us, length us, event | category | flops | bytes accessed | tf_op | source)
XLA Modules:
  0.0 474.3 jit_solution(2319376831182612432)
XLA Ops:
  8.0 0.0 copy-start
  8.0 0.0 all-reduce.3.cloned.1.call-start
  8.1 1.5 copy-done
  9.6 0.0 copy-start.2
  9.6 1.9 fusion
  11.5 0.7 copy.21
  12.1 0.0 copy-done.2
  12.1 2.4 convolution_bitcast_fusion
  14.5 0.0 all-reduce.3.cloned.1.call-update
  14.5 0.0 all-gather.5.cloned.1.call-start
  14.6 0.5 all-gather.5.cloned.1.call-update
  15.1 0.0 all-gather.3.cloned.1.call-start
  15.2 0.5 all-gather.3.cloned.1.call-update
  15.7 0.0 reduce-scatter.2.cloned.1.call-start
  15.7 25.1 %fusion.16 = f32[512,8192]{1,0:T(8,128)} fusion(bf16[512,2048]{1,0:T(8,128)(2,1)S(1)} %copy-done, bf16[8192,2048]{1,0:T(8,128)(2,1)} %param.8), kind=kOutput, calls=%fused_computation.25 | convolution fusion | flops 17179869184 | bytes 52428800 | tf_op jit(solution)/shard_map/dot_general | solution.py:29
  40.8 0.0 copy-start.3
  40.8 0.0 reduce-scatter.2.cloned.1.call-update
  40.9 0.6 copy-done.3
  41.5 0.1 fusion.6
  41.6 11.3 %all-reduce.3.cloned.1.call-done = (f32[2,256,64]{1,2,0:T(8,128)}, f32[512,64]{0,1:T(8,128)}) async-done(((f32[2,256,64]{1,2,0:T(8,128)}, f32[512,64]{0,1:T(8,128)}), (f32[2,256,64]{1,2,0:T(8,128)}, f32[512,64]{0,1:T(8,128)})) %all-reduce.3.cloned.1.call-update) | async-done | bytes 262160 | tf_op jit(solution)/shard_map/psum | solution.py:27
  52.9 0.9 broadcast_multiply_fusion
  53.9 1.2 fusion.3
  55.0 0.1 reshape.41
  55.1 0.0 all-gather.5.cloned.1.call-done
  55.2 4.1 fusion.17
  59.3 178.5 %all-gather.3.cloned.1.call-done = bf16[512,8192]{1,0:T(8,128)(2,1)} async-done(((bf16[512,2048]{1,0:T(8,128)(2,1)}), bf16[512,8192]{1,0:T(8,128)(2,1)}) %all-gather.3.cloned.1.call-update) | async-done | bytes 8388624 | tf_op jit(solution)/shard_map/all_gather | solution.py:21
  237.8 0.0 copy-start.1
  237.8 25.0 %convolution_convert_fusion = bf16[512,2048]{1,0:T(8,128)(2,1)} fusion(bf16[512,8192]{1,0:T(8,128)(2,1)} %all-gather.3.cloned.1.call-done, bf16[8192,2048]{1,0:T(8,128)(2,1)} %param.8), kind=kOutput, calls=%fused_computation | convolution fusion | flops 17180917760 | bytes 44040192 | tf_op jit(solution)/shard_map/dot_general | solution.py:20
  262.8 200.2 %reduce-scatter.2.cloned.1.call-done = f32[512,2048]{1,0:T(8,128)} async-done(((f32[512,8192]{1,0:T(8,128)}), f32[512,2048]{1,0:T(8,128)}) %reduce-scatter.2.cloned.1.call-update) | async-done | bytes 4194320 | tf_op jit(solution)/shard_map/reduce_scatter | solution.py:32
  463.0 3.8 convert_element_type.11
  466.8 0.0 copy-done.1
  (1 shorter events, 0.0 us)
Async XLA Ops:
  8.0 1.6 copy-start
  8.0 44.9 %all-reduce.3.cloned.1.call-start = ((), (), s32[]{:S(2)}) async-start(), calls=%async_computation.4 | async-start | bytes 524288 | tf_op jit(solution)/shard_map/psum | solution.py:27
  9.6 2.5 copy-start.2
  14.5 40.6 %all-gather.5.cloned.1.call-start = ((), (), s32[]{:S(2)}) async-start(), calls=%async_computation.3 | async-start | bytes 2621440 | tf_op jit(solution)/shard_map/all_gather | solution.py:52
  15.1 222.7 %all-gather.3.cloned.1.call-start = ((), (), s32[]{:S(2)}) async-start(), calls=%async_computation.1 | async-start | bytes 10485760 | tf_op jit(solution)/shard_map/all_gather | solution.py:21
  15.7 447.3 %reduce-scatter.2.cloned.1.call-start = ((), (), s32[]{:S(2)}) async-start(), calls=%async_computation.2 | async-start | bytes 20971520 | tf_op jit(solution)/shard_map/reduce_scatter | solution.py:32
  40.8 0.7 copy-start.3
  237.8 229.0 %copy-start.1 = (bf16[512,2048]{1,0:T(8,128)(2,1)S(1)}, bf16[512,2048]{1,0:T(8,128)(2,1)}, u32[]{:S(2)}) copy-start(bf16[512,2048]{1,0:T(8,128)(2,1)} %param.9) | copy-start | bytes 6291460
Sparse Core Ops, SparseCore 0:
  14.6 38.2 all-reduce.2
  55.4 407.5 reduce-scatter.1
Sparse Core Ops, SparseCore 1:
  16.6 25.1 all-gather.4
  43.2 194.6 all-gather.2
where the time goes:
time: 475 us; the launch traced here: 474 us
  waiting for transfers between devices  391 us (82%)
  matrix products  59.6 us (13%)
  between operations  15.5 us (3%)
  other arithmetic  4.85 us (1%)
    reduce_scatter x1, waiting for transfers between devices, per_device(): lax.psum_scatter(grad_term_full, 'mp', scatter_dimension=1, tiled=True)  200 us
    all_gather x1, waiting for transfers between devices, per_device(): lax.all_gather(attn_out, 'mp', axis=1, tiled=True)  179 us
    dot_general x1, matrix products, per_device(): lax.dot_general(cotangent, out_weight, (((1,), (1,)), ((), ())), preferre...  25.1 us
    dot_general x1, matrix products, per_device(): jnp.dot(lax.all_gather(attn_out, 'mp', axis=1, tiled=True), out_weight, p...  25 us
    psum x1, waiting for transfers between devices, per_device(): proj_in, proj_out = lax.psum((part_in, part_out), 'mp')  11.3 us
  transfers between devices with their start and end apart: 4, of which 3 were waited for; matrix products, arithmetic and copies ran while one was open for 12% of the time, Pallas kernels for 0%

commit v1 on v0

v1 whole, which is shorter than its diff:
```python
import functools

import jax
import jax.numpy as jnp
from jax import lax
from jax.experimental import pallas as pl
from jax.experimental.pallas import tpu as pltpu
from jax.sharding import PartitionSpec as P

LEN = 256
CHUNKS = 2
STEPS = 32767.0
MESH = pl.DeviceIdType.MESH

HIGHEST_PRECISION = lax.Precision.HIGHEST


def kernel(n, narrow, attn_hbm, cot_hbm, w_hbm, lay_ref, grad_ref, gath, cot, wbuf, acc, gacc, tmp, rs, stage,
           sc, sstage, in_sem, w_sem, ag_recv, ag_send_r, ag_send_l, rs_recv, rs_send, sc_recv, sc_send):
    me = lax.axis_index("mp")
    tok, bw = cot.shape
    cr = tok // CHUNKS
    tn = min(256, bw)
    tiles = bw // tn

    def rows_of(c):
        return pl.ds(pl.multiple_of(c * cr, cr), cr)

    def cols_of(t):
        return pl.ds(pl.multiple_of(t * tn, tn), tn)

    def w_load(block, slot):
        return pltpu.make_async_copy(
            w_hbm.at[pl.ds(pl.multiple_of(block * bw, bw), bw), :], wbuf.at[slot], w_sem.at[slot])

    attn_in = pltpu.make_async_copy(attn_hbm, gath.at[me], in_sem.at[0])
    cot_in = pltpu.make_async_copy(cot_hbm, cot, in_sem.at[1])
    attn_in.start()
    cot_in.start()

    barrier = pltpu.get_barrier_semaphore()
    has_left, has_right = me > 0, me < n - 1

    @pl.when(has_left)
    def _():
        pl.semaphore_signal(barrier, inc=1, device_id={"mp": me - 1}, device_id_type=MESH)

    @pl.when(has_right)
    def _():
        pl.semaphore_signal(barrier, inc=1, device_id={"mp": me + 1}, device_id_type=MESH)

    pl.semaphore_wait(barrier, has_left.astype(jnp.int32) + has_right.astype(jnp.int32))

    def ag_copy(origin, c, side):
        part = gath.at[origin, rows_of(c)]
        sems = ag_send_r if side > 0 else ag_send_l
        return pltpu.make_async_remote_copy(
            src_ref=part, dst_ref=part, send_sem=sems.at[origin, c], recv_sem=ag_recv.at[origin, c],
            device_id={"mp": me + side}, device_id_type=MESH)

    def ag_wait(origin, c):
        part = gath.at[origin, rows_of(c)]
        pltpu.make_async_copy(part, part, ag_recv.at[origin, c]).wait()

    def rs_copies(d, c, side):
        out = d - 1 if side > 0 else d
        there = d if side > 0 else jnp.where(d == me - 1, n, d)
        data = pltpu.make_async_remote_copy(
            src_ref=stage.at[out, rows_of(c)], dst_ref=rs.at[there, rows_of(c)],
            send_sem=rs_send.at[out, c], recv_sem=rs_recv.at[there, c],
            device_id={"mp": me + side}, device_id_type=MESH)
        if not narrow:
            return (data,)
        return (data, pltpu.make_async_remote_copy(
            src_ref=sstage.at[out, c], dst_ref=sc.at[there, c],
            send_sem=sc_send.at[out, c], recv_sem=sc_recv.at[there, c],
            device_id={"mp": me + side}, device_id_type=MESH))

    def rs_wait(slot, c):
        pltpu.make_async_copy(rs.at[slot, rows_of(c)], rs.at[slot, rows_of(c)], rs_recv.at[slot, c]).wait()
        if narrow:
            pltpu.make_async_copy(sc.at[slot, c], sc.at[slot, c], sc_recv.at[slot, c]).wait()

    def scale_of(slot, c):
        wide = jnp.broadcast_to(sc[slot, c][0:1, :], (128, cr))
        return jnp.transpose(wide)[:, 0:1] * (1.0 / STEPS)

    attn_in.wait()
    for c in range(CHUNKS):
        @pl.when(has_right)
        def _():
            ag_copy(me, c, 1).start()

        @pl.when(has_left)
        def _():
            ag_copy(me, c, -1).start()
    cot_in.wait()

    def partial_tile(slot, rows, t):
        return lax.dot_general(
            cot[rows, :], wbuf[slot, cols_of(t), :], (((1,), (1,)), ((), ())),
            preferred_element_type=jnp.float32)

    def rs_task(d, c, side, slot, incoming):
        rows = rows_of(c)
        src = d

        def first(t, top):
            tmp[:, cols_of(t)] = partial_tile(slot, rows, t)
            return top

        lax.fori_loop(0, tiles, first, 0)

        @pl.when(incoming)
        def _():
            rs_wait(src, c)
            scale = scale_of(src, c) if narrow else 1.0

            def add(t, top):
                tmp[:, cols_of(t)] += rs[src, rows, cols_of(t)].astype(jnp.float32) * scale
                return top

            lax.fori_loop(0, tiles, add, 0)

        out = d - 1 if side > 0 else d
        if narrow:
            def most(t, top):
                part = jnp.abs(tmp[:, cols_of(t)])
                for k in range(tn // 128):
                    top = jnp.maximum(top, part[:, k * 128:(k + 1) * 128])
                return top

            top = lax.fori_loop(0, tiles, most, jnp.full((cr, 128), 1e-30, jnp.float32))
            sstage[out, c] = jnp.broadcast_to(jnp.max(jnp.transpose(top), axis=0, keepdims=True), (8, cr))
            inv = STEPS / jnp.max(top, axis=1, keepdims=True)

            def code(t, top):
                stage[out, rows, cols_of(t)] = jnp.round(tmp[:, cols_of(t)] * inv).astype(jnp.int32).astype(jnp.int16)
                return top
        else:
            def code(t, top):
                stage[out, rows, cols_of(t)] = tmp[:, cols_of(t)]
                return top

        lax.fori_loop(0, tiles, code, 0)
        for copy in rs_copies(d, c, side):
            copy.start()

    def rs_last(c, slot):
        rows = rows_of(c)
        rs_wait(slot, c)
        scale = scale_of(slot, c) if narrow else 1.0

        def add(t, top):
            gacc[rows, cols_of(t)] += rs[slot, rows, cols_of(t)].astype(jnp.float32) * scale
            return top

        lax.fori_loop(0, tiles, add, 0)

    def forward(origin, slot, fresh=False):
        def body(t, top):
            part = jnp.dot(gath[origin], wbuf[slot, :, cols_of(t)], preferred_element_type=jnp.float32)
            if fresh:
                acc[:, cols_of(t)] = part
            else:
                acc[:, cols_of(t)] += part
            return top

        lax.fori_loop(0, tiles, body, 0)

    def own():
        load = w_load(me, 0)
        load.start()
        load.wait()

        def body(t, top):
            gacc[:, cols_of(t)] = partial_tile(0, slice(None), t)
            return top

        lax.fori_loop(0, tiles, body, 0)
        forward(me, 0, True)

    def ring(r, top):
        from_left, from_right = me - r, me + r
        ag_l, ag_r = (r > 0) & (from_left >= 0), (r > 0) & (from_right < n)
        d_r = jnp.where(has_left, n - r, n - 1 - r)
        d_l = jnp.where(has_right, r - 1, r)
        turn = (r > 0)
        send_r = has_right & (d_r > me) & (turn | (me == 0))
        send_l = has_left & (d_l < me) & (turn | (me == n - 1))
        last_r = has_left & turn & (d_r == me)
        last_l = has_right & turn & (d_l == me)

        @pl.when(send_r)
        def _():
            w_load(d_r, 0).start()

        @pl.when(send_l)
        def _():
            w_load(d_l, 1).start()

        @pl.when(send_r)
        def _():
            w_load(d_r, 0).wait()

        @pl.when(send_l)
        def _():
            w_load(d_l, 1).wait()

        def chunk(c, top):
            @pl.when(ag_l)
            def _():
                ag_wait(from_left, c)

                @pl.when(has_right)
                def _():
                    ag_copy(from_left, c, 1).start()

            @pl.when(ag_r)
            def _():
                ag_wait(from_right, c)

                @pl.when(has_left)
                def _():
                    ag_copy(from_right, c, -1).start()

            @pl.when(send_r)
            def _():
                rs_task(d_r, c, 1, 0, has_left)

            @pl.when(send_l)
            def _():
                rs_task(d_l, c, -1, 1, has_right)

            return top

        lax.fori_loop(0, CHUNKS, chunk, 0)

        @pl.when(ag_l)
        def _():
            w_load(from_left, 0).start()

        @pl.when(ag_r)
        def _():
            w_load(from_right, 1).start()

        @pl.when(r == 0)
        def _():
            own()

        @pl.when(ag_l)
        def _():
            w_load(from_left, 0).wait()
            forward(from_left, 0)

        @pl.when(ag_r)
        def _():
            w_load(from_right, 1).wait()
            forward(from_right, 1)

        def finish(c, top):
            @pl.when(last_r)
            def _():
                rs_last(c, me)

            @pl.when(last_l)
            def _():
                rs_last(c, n)

            return top

        lax.fori_loop(0, CHUNKS, finish, 0)
        return top

    lax.fori_loop(0, n, ring, 0)

    def result(t, top):
        lay_ref[:, cols_of(t)] = acc[:, cols_of(t)].astype(lay_ref.dtype)
        grad_ref[:, cols_of(t)] = gacc[:, cols_of(t)].astype(grad_ref.dtype)
        return top

    lax.fori_loop(0, tiles, result, 0)

    def drain(o, top):
        for c in range(CHUNKS):
            @pl.when(has_right & (o <= me))
            def _():
                ag_copy(o, c, 1).wait_send()

            @pl.when(has_left & (o >= me))
            def _():
                ag_copy(o, c, -1).wait_send()

            @pl.when(o > me)
            def _():
                for copy in rs_copies(o, c, 1):
                    copy.wait_send()

            @pl.when(o < me)
            def _():
                for copy in rs_copies(o, c, -1):
                    copy.wait_send()
        return top

    lax.fori_loop(0, n, drain, 0)


def both_products(n, attn_out, cotangent, out_weight):
    tok, bw = attn_out.shape
    narrow = n <= 8
    wire = jnp.int16 if narrow else jnp.float32
    cr = tok // CHUNKS
    dma = pltpu.SemaphoreType.DMA
    out = jax.ShapeDtypeStruct((tok, bw), jnp.bfloat16)
    return pl.pallas_call(
        functools.partial(kernel, n, narrow),
        out_shape=(out, out),
        in_specs=[pl.BlockSpec(memory_space=pl.ANY)] * 3,
        out_specs=(pl.BlockSpec(memory_space=pltpu.VMEM),) * 2,
        scratch_shapes=[
            pltpu.VMEM((n, tok, bw), jnp.bfloat16),
            pltpu.VMEM((tok, bw), jnp.bfloat16),
            pltpu.VMEM((2, bw, bw), jnp.bfloat16),
            pltpu.VMEM((tok, bw), jnp.float32),
            pltpu.VMEM((tok, bw), jnp.float32),
            pltpu.VMEM((cr, bw), jnp.float32),
            pltpu.VMEM((n + 1, tok, bw), wire),
            pltpu.VMEM((n - 1, tok, bw), wire),
            pltpu.VMEM((n + 1, CHUNKS, 8, cr), jnp.float32),
            pltpu.VMEM((n - 1, CHUNKS, 8, cr), jnp.float32),
            dma((2,)),
            dma((2,)),
            dma((n, CHUNKS)),
            dma((n, CHUNKS)),
            dma((n, CHUNKS)),
            dma((n + 1, CHUNKS)),
            dma((n - 1, CHUNKS)),
            dma((n + 1, CHUNKS)),
            dma((n - 1, CHUNKS)),
        ],
        compiler_params=pltpu.CompilerParams(
            collective_id=0, has_side_effects=True, vmem_limit_bytes=62 * 1024 * 1024
        ),
        cost_estimate=pl.CostEstimate(
            flops=4 * n * tok * bw * bw, bytes_accessed=400 * 1024 * 1024, transcendentals=0
        ),
    )(attn_out, cotangent, out_weight)


def per_device(n, attn_out, out_weight, cotangent, proj_in_w, proj_out_w, queries, lengths):
    tok_rows = attn_out.shape[0]
    block_width = attn_out.shape[1]
    rank_width = proj_in_w.shape[1]
    seq_count = lengths.shape[0]
    block_start = lax.axis_index("mp") * block_width
    local_in_w = lax.dynamic_slice_in_dim(proj_in_w, block_start, block_width, 0)
    local_out_w = lax.dynamic_slice_in_dim(proj_out_w, block_start, block_width, 0)
    part_in = jnp.dot(attn_out, local_in_w, preferred_element_type=jnp.float32)
    part_out = jnp.dot(cotangent, local_out_w, preferred_element_type=jnp.float32)
    proj_in, proj_out = lax.psum((part_in, part_out), "mp")
    layer_out, grad_in = both_products(n, attn_out, cotangent, out_weight)
    slot_index = jnp.arange(tok_rows, dtype=jnp.int32)
    example_ids = slot_index // LEN
    offsets = slot_index % LEN
    seq_slots = jnp.arange(seq_count, dtype=jnp.int32)
    live_table = (example_ids[:, None] == seq_slots[None, :]) & (
        offsets[:, None] < lengths[None, :]
    )
    live_rows = jnp.sum(live_table.astype(jnp.float32), axis=1)
    weighted = (proj_in * live_rows[:, None]).reshape(seq_count, LEN, rank_width)
    kronecker = jnp.einsum(
        "eti,etj->eij",
        weighted,
        proj_out.reshape(seq_count, LEN, rank_width),
        precision=HIGHEST_PRECISION,
    ).reshape(seq_count, rank_width * rank_width)
    scores = lax.dot_general(
        kronecker,
        lax.all_gather(queries, "dp", axis=1, tiled=True).astype(jnp.float32),
        (((1,), (1,)), ((), ())),
        precision=HIGHEST_PRECISION,
        preferred_element_type=jnp.float32,
    )
    return (layer_out, grad_in, scores)


def solution(mesh):
    in_specs = (
        P(("groups", "dp"), "mp"),
        P(None, "mp"),
        P(("groups", "dp"), "mp"),
        P(),
        P(),
        P("mp", "dp"),
        P(("groups", "dp")),
    )
    out_specs = (P(("groups", "dp"), "mp"), P(("groups", "dp"), "mp"), P(("groups", "dp"), "mp"))
    return jax.shard_map(
        functools.partial(per_device, mesh.shape["mp"]),
        mesh=mesh, in_specs=in_specs, out_specs=out_specs, check_vma=False,
    )
```

time: 475 us -> 316 us (0.67)
  waiting for transfers between devices: 391 us -> 0.57 us
  Pallas kernels: 0 us -> 280 us
  matrix products: 59.6 us -> 9.78 us
    pallas_call x0 -> x1, Pallas kernels: none -> 280 us  [both_products(): pl.pallas_call(functools.partial(kernel, n, narrow), out_shape=(out, out)...]
    reduce_scatter x1 -> x0, waiting for transfers between devices: 200 us -> none  [per_device(): lax.psum_scatter(grad_term_full, 'mp', scatter_dimension=1, tiled=True)]
    all_gather x1 -> x0, waiting for transfers between devices: 179 us -> none  [per_device(): lax.all_gather(attn_out, 'mp', axis=1, tiled=True)]
    dot_general x2 -> x0, matrix products: 50.1 us -> none  [the longest x1 25.1 us: per_device(): lax.dot_general(cotangent, out_weight, (((1,), (1,)), ((), ())), preferre...]
    psum x1, waiting for transfers between devices: 11.3 us -> 0.01 us  [per_device(): proj_in, proj_out = lax.psum((part_in, part_out), 'mp')]
  transfers between devices with their start and end apart: 4 -> 2, of which waited for: 3 -> 0; matrix products, arithmetic and copies ran while one was open for 12% -> 1% of each run, Pallas kernels for 0% -> 90%
where the time goes in v1:
time: 316 us; the launch traced here: 312 us
  Pallas kernels  280 us (89%)
  between operations  15.6 us (5%)
  matrix products  9.78 us (3%)
  local copies, waits for them, and re-layouts  5.61 us (2%)
    pallas_call x1, Pallas kernels, both_products(): pl.pallas_call(functools.partial(kernel, n, narrow), out_shape=(out, out)...  280 us
  transfers between devices with their start and end apart: 2, of which 0 were waited for; matrix products, arithmetic and copies ran while one was open for 1% of the time, Pallas kernels for 90%

profile of v1, /device:TPU:0, one launch (start us, length us, event | category | flops | bytes accessed | tf_op | source)
XLA Modules:
  0.0 312.3 jit_solution(8517170230132210147)
XLA Ops:
  8.0 0.0 copy-start
  8.0 0.0 copy-start.1
  8.0 0.0 all-reduce.3.cloned.1.call-start
  8.1 1.2 copy-done
  9.2 2.3 fusion
  11.6 0.7 copy.21
  12.2 0.0 copy-done.1
  12.2 2.4 convolution_bitcast_fusion
  14.6 0.0 all-reduce.3.cloned.1.call-update
  14.6 0.0 all-gather.2.cloned.1.call-start
  14.7 0.5 all-gather.2.cloned.1.call-update
  15.2 0.0 copy-start.4
  15.2 279.5 %shard_map.94 = (bf16[512,2048]{1,0:T(8,128)(2,1)}, bf16[512,2048]{1,0:T(8,128)(2,1)}) custom-call(bf16[512,2048]{1,0:T(8,128)(2,1)} %attn_hbm.1, bf16[512,2048]{1,0:T(8,128)(2,1)} %cot_hbm.1, bf16[8192,2048]{1,0:T(8,128)(2,1)} %w_hbm.1), custom_call_target="tpu_custom_call" | custom-call | flops 34359738368 | bytes 419430400 | tf_op jit(solution)/shard_map/pallas_call | solution.py:315
  294.8 0.0 copy-start.3
  294.8 0.0 copy-done.4
  294.8 0.1 fusion.6
  294.9 0.0 all-reduce.3.cloned.1.call-done
  294.9 1.0 broadcast_multiply_fusion
  295.9 1.2 fusion.3
  297.1 0.1 reshape.41
  297.2 0.0 all-gather.2.cloned.1.call-done
  297.2 3.9 %fusion.16 = f32[2,256]{1,0:T(2,128)} fusion(f32[2,4096]{1,0:T(2,128)S(1)} %reshape.41, bf16[256,4096]{1,0:T(8,128)(2,1)} %all-gather.2.cloned.1.call-done), kind=kOutput, calls=%fused_computation.24 | convolution fusion | flops 25165824 | bytes 2131968 | tf_op jit(solution)/shard_map/dot_general | solution.py:377
  301.2 0.0 copy-done.3
  301.2 0.0 copy-start.2
  301.2 1.3 copy.26
  302.5 1.0 copy-done.2
  303.5 1.3 copy.27
  (1 shorter events, 0.0 us)
Async XLA Ops:
  8.0 1.2 copy-start
  8.0 4.2 %copy-start.1 = (bf16[512,2048]{1,0:T(8,128)(2,1)S(1)}, bf16[512,2048]{1,0:T(8,128)(2,1)}, u32[]{:S(2)}) copy-start(bf16[512,2048]{1,0:T(8,128)(2,1)} %attn_hbm.1) | copy-start | bytes 6291460
  8.0 286.9 %all-reduce.3.cloned.1.call-start = ((), (), s32[]{:S(2)}) async-start(), calls=%async_computation.1 | async-start | bytes 524288 | tf_op jit(solution)/shard_map/psum | solution.py:360
  14.6 282.6 %all-gather.2.cloned.1.call-start = ((), (), s32[]{:S(2)}) async-start(), calls=%async_computation | async-start | bytes 2621440 | tf_op jit(solution)/shard_map/all_gather | solution.py:379
  15.2 279.6 %copy-start.4 = (s32[2]{0:T(128)S(1)}, s32[2]{0:T(128)}, u32[]{:S(2)}) copy-start(s32[2]{0:T(128)} %param.13) | copy-start | bytes 28
  294.8 6.4 %copy-start.3 = (bf16[512,2048]{1,0:T(8,128)(2,1)S(1)}, bf16[512,2048]{1,0:T(8,128)(2,1)}, u32[]{:S(2)}) copy-start(bf16[512,2048]{1,0:T(8,128)(2,1)} %get-tuple-element.14) | copy-start | bytes 6291460
  301.2 2.3 copy-start.2
Sparse Core Ops, SparseCore 0:
  14.8 41.4 all-reduce.2
Sparse Core Ops, SparseCore 1:
  16.8 25.1 all-gather.1

commit v2 on v1

--- a/solution.py
+++ b/solution.py
@@ -8,7 +8,7 @@
 from jax.sharding import PartitionSpec as P
 
 LEN = 256
-CHUNKS = 2
+CHUNKS = 4
 STEPS = 32767.0
 MESH = pl.DeviceIdType.MESH
 
@@ -101,7 +101,7 @@
             cot[rows, :], wbuf[slot, cols_of(t), :], (((1,), (1,)), ((), ())),
             preferred_element_type=jnp.float32)
 
-    def rs_task(d, c, side, slot, incoming):
+    def rs_task(d, c, side, slot, incoming, opening):
         rows = rows_of(c)
         src = d
 
@@ -143,6 +143,16 @@
                 return top
 
         lax.fori_loop(0, tiles, code, 0)
+
+        @pl.when(opening)
+        def _():
+            ag_copy(0 if side > 0 else n - 1, c, side).wait_send()
+
+        @pl.when(jnp.logical_not(opening))
+        def _():
+            for copy in rs_copies(d + side, c, side):
+                copy.wait_send()
+
         for copy in rs_copies(d, c, side):
             copy.start()
 
@@ -183,13 +193,11 @@
     def ring(r, top):
         from_left, from_right = me - r, me + r
         ag_l, ag_r = (r > 0) & (from_left >= 0), (r > 0) & (from_right < n)
-        d_r = jnp.where(has_left, n - r, n - 1 - r)
-        d_l = jnp.where(has_right, r - 1, r)
-        turn = (r > 0)
-        send_r = has_right & (d_r > me) & (turn | (me == 0))
-        send_l = has_left & (d_l < me) & (turn | (me == n - 1))
-        last_r = has_left & turn & (d_r == me)
-        last_l = has_right & turn & (d_l == me)
+        late_r, late_l = r - me, r - (n - 1 - me)
+        d_r, d_l = n - 1 - late_r, late_l
+        send_r = (late_r >= 0) & (d_r > me)
+        send_l = (late_l >= 0) & (d_l < me)
+        last = r == n - 1
 
         @pl.when(send_r)
         def _():
@@ -199,21 +207,14 @@
         def _():
             w_load(d_l, 1).start()
 
-        @pl.when(send_r)
-        def _():
-            w_load(d_r, 0).wait()
-
-        @pl.when(send_l)
-        def _():
-            w_load(d_l, 1).wait()
-
-        def chunk(c, top):
+        def pass_on(c, top):
             @pl.when(ag_l)
             def _():
                 ag_wait(from_left, c)
 
                 @pl.when(has_right)
                 def _():
+                    ag_copy(from_left + 1, c, 1).wait_send()
                     ag_copy(from_left, c, 1).start()
 
             @pl.when(ag_r)
@@ -222,15 +223,29 @@
 
                 @pl.when(has_left)
                 def _():
+                    ag_copy(from_right - 1, c, -1).wait_send()
                     ag_copy(from_right, c, -1).start()
 
+            return top
+
+        lax.fori_loop(0, CHUNKS, pass_on, 0)
+
+        @pl.when(send_r)
+        def _():
+            w_load(d_r, 0).wait()
+
+        @pl.when(send_l)
+        def _():
+            w_load(d_l, 1).wait()
+
+        def chunk(c, top):
             @pl.when(send_r)
             def _():
-                rs_task(d_r, c, 1, 0, has_left)
+                rs_task(d_r, c, 1, 0, has_left, late_r == 0)
 
             @pl.when(send_l)
             def _():
-                rs_task(d_l, c, -1, 1, has_right)
+                rs_task(d_l, c, -1, 1, has_right, late_l == 0)
 
             return top
 
@@ -243,10 +258,6 @@
         @pl.when(ag_r)
         def _():
             w_load(from_right, 1).start()
-
-        @pl.when(r == 0)
-        def _():
-            own()
 
         @pl.when(ag_l)
         def _():
@@ -259,11 +270,11 @@
             forward(from_right, 1)
 
         def finish(c, top):
-            @pl.when(last_r)
+            @pl.when(last & has_left)
             def _():
                 rs_last(c, me)
 
-            @pl.when(last_l)
+            @pl.when(last & has_right)
             def _():
                 rs_last(c, n)
 
@@ -272,6 +283,7 @@
         lax.fori_loop(0, CHUNKS, finish, 0)
         return top
 
+    own()
     lax.fori_loop(0, n, ring, 0)
 
     def result(t, top):
@@ -281,28 +293,16 @@
 
     lax.fori_loop(0, tiles, result, 0)
 
-    def drain(o, top):
-        for c in range(CHUNKS):
-            @pl.when(has_right & (o <= me))
-            def _():
-                ag_copy(o, c, 1).wait_send()
-
-            @pl.when(has_left & (o >= me))
-            def _():
-                ag_copy(o, c, -1).wait_send()
-
-            @pl.when(o > me)
-            def _():
-                for copy in rs_copies(o, c, 1):
-                    copy.wait_send()
-
-            @pl.when(o < me)
-            def _():
-                for copy in rs_copies(o, c, -1):
-                    copy.wait_send()
-        return top
-
-    lax.fori_loop(0, n, drain, 0)
+    for c in range(CHUNKS):
+        @pl.when(has_right)
+        def _():
+            for copy in rs_copies(me + 1, c, 1):
+                copy.wait_send()
+
+        @pl.when(has_left)
+        def _():
+            for copy in rs_copies(me - 1, c, -1):
+                copy.wait_send()
 
 
 def both_products(n, attn_out, cotangent, out_weight):

time: 316 us -> 249 us (0.79)
  Pallas kernels: 280 us -> 216 us
    pallas_call x1, Pallas kernels: 280 us -> 216 us  [both_products(): pl.pallas_call(functools.partial(kernel, n, narrow), out_shape=(out, out)...]
  transfers between devices with their start and end apart: 2 -> 2, of which waited for: 0 -> 0; matrix products, arithmetic and copies ran while one was open for 1% -> 1% of each run, Pallas kernels for 90% -> 87%
where the time goes in v2:
time: 249 us; the launch traced here: 248 us
  Pallas kernels  216 us (87%)
  between operations  15.6 us (6%)
  matrix products  9.78 us (4%)
  local copies, waits for them, and re-layouts  5.61 us (2%)
    pallas_call x1, Pallas kernels, both_products(): pl.pallas_call(functools.partial(kernel, n, narrow), out_shape=(out, out)...  216 us
  transfers between devices with their start and end apart: 2, of which 0 were waited for; matrix products, arithmetic and copies ran while one was open for 1% of the time, Pallas kernels for 87%

profile of v2, /device:TPU:0, one launch (start us, length us, event | category | flops | bytes accessed | tf_op | source)
XLA Modules:
  0.0 248.4 jit_solution(5710288542345343815)
XLA Ops:
  8.0 0.0 copy-start
  8.0 0.0 copy-start.1
  8.0 0.0 all-reduce.3.cloned.1.call-start
  8.1 1.2 copy-done
  9.2 2.3 fusion
  11.6 0.7 copy.21
  12.2 0.0 copy-done.1
  12.2 2.4 convolution_bitcast_fusion
  14.6 0.0 all-reduce.3.cloned.1.call-update
  14.6 0.0 all-gather.2.cloned.1.call-start
  14.7 0.5 all-gather.2.cloned.1.call-update
  15.2 0.0 copy-start.4
  15.2 215.6 %shard_map.94 = (bf16[512,2048]{1,0:T(8,128)(2,1)}, bf16[512,2048]{1,0:T(8,128)(2,1)}) custom-call(bf16[512,2048]{1,0:T(8,128)(2,1)} %attn_hbm.1, bf16[512,2048]{1,0:T(8,128)(2,1)} %cot_hbm.1, bf16[8192,2048]{1,0:T(8,128)(2,1)} %w_hbm.1), custom_call_target="tpu_custom_call" | custom-call | flops 34359738368 | bytes 419430400 | tf_op jit(solution)/shard_map/pallas_call | solution.py:315
  230.9 0.0 copy-start.3
  230.9 0.0 copy-done.4
  230.9 0.1 fusion.6
  231.0 0.0 all-reduce.3.cloned.1.call-done
  231.0 1.0 broadcast_multiply_fusion
  232.0 1.2 fusion.3
  233.2 0.1 reshape.41
  233.3 0.0 all-gather.2.cloned.1.call-done
  233.3 3.9 %fusion.16 = f32[2,256]{1,0:T(2,128)} fusion(f32[2,4096]{1,0:T(2,128)S(1)} %reshape.41, bf16[256,4096]{1,0:T(8,128)(2,1)} %all-gather.2.cloned.1.call-done), kind=kOutput, calls=%fused_computation.24 | convolution fusion | flops 25165824 | bytes 2131968 | tf_op jit(solution)/shard_map/dot_general | solution.py:377
  237.2 0.0 copy-done.3
  237.2 0.0 copy-start.2
  237.3 1.3 copy.26
  238.6 1.0 copy-done.2
  239.6 1.3 copy.27
  (1 shorter events, 0.0 us)
Async XLA Ops:
  8.0 1.2 copy-start
  8.0 4.2 %copy-start.1 = (bf16[512,2048]{1,0:T(8,128)(2,1)S(1)}, bf16[512,2048]{1,0:T(8,128)(2,1)}, u32[]{:S(2)}) copy-start(bf16[512,2048]{1,0:T(8,128)(2,1)} %attn_hbm.1) | copy-start | bytes 6291460
  8.0 223.0 %all-reduce.3.cloned.1.call-start = ((), (), s32[]{:S(2)}) async-start(), calls=%async_computation.1 | async-start | bytes 524288 | tf_op jit(solution)/shard_map/psum | solution.py:360
  14.6 218.7 %all-gather.2.cloned.1.call-start = ((), (), s32[]{:S(2)}) async-start(), calls=%async_computation | async-start | bytes 2621440 | tf_op jit(solution)/shard_map/all_gather | solution.py:379
  15.2 215.7 %copy-start.4 = (s32[2]{0:T(128)S(1)}, s32[2]{0:T(128)}, u32[]{:S(2)}) copy-start(s32[2]{0:T(128)} %param.13) | copy-start | bytes 28
  230.9 6.4 %copy-start.3 = (bf16[512,2048]{1,0:T(8,128)(2,1)S(1)}, bf16[512,2048]{1,0:T(8,128)(2,1)}, u32[]{:S(2)}) copy-start(bf16[512,2048]{1,0:T(8,128)(2,1)} %get-tuple-element.14) | copy-start | bytes 6291460
  237.2 2.3 copy-start.2
Sparse Core Ops, SparseCore 0:
  14.8 41.6 all-reduce.2
Sparse Core Ops, SparseCore 1:
  16.8 25.1 all-gather.1

commit v3 on v2

--- a/solution.py
+++ b/solution.py
@@ -15,7 +15,7 @@
 HIGHEST_PRECISION = lax.Precision.HIGHEST
 
 
-def kernel(n, narrow, attn_hbm, cot_hbm, w_hbm, lay_ref, grad_ref, gath, cot, wbuf, acc, gacc, tmp, rs, stage,
+def kernel(n, narrow, attn_hbm, cot_hbm, w_hbm, pw_ref, lay_ref, grad_ref, pin_ref, gath, cot, wbuf, acc, gacc, tmp, rs, stage,
            sc, sstage, in_sem, w_sem, ag_recv, ag_send_r, ag_send_l, rs_recv, rs_send, sc_recv, sc_send):
     me = lax.axis_index("mp")
     tok, bw = cot.shape
@@ -177,6 +177,13 @@
             return top
 
         lax.fori_loop(0, tiles, body, 0)
+        proj = lax.dot_general(
+            gath[origin], pw_ref[:, pl.ds(pl.multiple_of(origin * bw, bw), bw)], (((1,), (1,)), ((), ())),
+            preferred_element_type=jnp.float32)
+        if fresh:
+            pin_ref[...] = proj
+        else:
+            pin_ref[...] += proj
 
     def own():
         load = w_load(me, 0)
@@ -197,7 +204,6 @@
         d_r, d_l = n - 1 - late_r, late_l
         send_r = (late_r >= 0) & (d_r > me)
         send_l = (late_l >= 0) & (d_l < me)
-        last = r == n - 1
 
         @pl.when(send_r)
         def _():
@@ -268,19 +274,6 @@
         def _():
             w_load(from_right, 1).wait()
             forward(from_right, 1)
-
-        def finish(c, top):
-            @pl.when(last & has_left)
-            def _():
-                rs_last(c, me)
-
-            @pl.when(last & has_right)
-            def _():
-                rs_last(c, n)
-
-            return top
-
-        lax.fori_loop(0, CHUNKS, finish, 0)
         return top
 
     own()
@@ -288,10 +281,29 @@
 
     def result(t, top):
         lay_ref[:, cols_of(t)] = acc[:, cols_of(t)].astype(lay_ref.dtype)
-        grad_ref[:, cols_of(t)] = gacc[:, cols_of(t)].astype(grad_ref.dtype)
         return top
 
     lax.fori_loop(0, tiles, result, 0)
+
+    def finish(c, top):
+        rows = rows_of(c)
+
+        @pl.when(has_left)
+        def _():
+            rs_last(c, me)
+
+        @pl.when(has_right)
+        def _():
+            rs_last(c, n)
+
+        def narrowed(t, top):
+            grad_ref[rows, cols_of(t)] = gacc[rows, cols_of(t)].astype(grad_ref.dtype)
+            return top
+
+        lax.fori_loop(0, tiles, narrowed, 0)
+        return top
+
+    lax.fori_loop(0, CHUNKS, finish, 0)
 
     for c in range(CHUNKS):
         @pl.when(has_right)
@@ -305,7 +317,7 @@
                 copy.wait_send()
 
 
-def both_products(n, attn_out, cotangent, out_weight):
+def both_products(n, attn_out, cotangent, out_weight, proj_in_t):
     tok, bw = attn_out.shape
     narrow = n <= 8
     wire = jnp.int16 if narrow else jnp.float32
@@ -314,9 +326,9 @@
     out = jax.ShapeDtypeStruct((tok, bw), jnp.bfloat16)
     return pl.pallas_call(
         functools.partial(kernel, n, narrow),
-        out_shape=(out, out),
-        in_specs=[pl.BlockSpec(memory_space=pl.ANY)] * 3,
-        out_specs=(pl.BlockSpec(memory_space=pltpu.VMEM),) * 2,
+        out_shape=(out, out, jax.ShapeDtypeStruct((tok, proj_in_t.shape[0]), jnp.float32)),
+        in_specs=[pl.BlockSpec(memory_space=pl.ANY)] * 3 + [pl.BlockSpec(memory_space=pltpu.VMEM)],
+        out_specs=(pl.BlockSpec(memory_space=pltpu.VMEM),) * 3,
         scratch_shapes=[
             pltpu.VMEM((n, tok, bw), jnp.bfloat16),
             pltpu.VMEM((tok, bw), jnp.bfloat16),
@@ -344,7 +356,7 @@
         cost_estimate=pl.CostEstimate(
             flops=4 * n * tok * bw * bw, bytes_accessed=400 * 1024 * 1024, transcendentals=0
         ),
-    )(attn_out, cotangent, out_weight)
+    )(attn_out, cotangent, out_weight, proj_in_t)
 
 
 def per_device(n, attn_out, out_weight, cotangent, proj_in_w, proj_out_w, queries, lengths):
@@ -353,12 +365,10 @@
     rank_width = proj_in_w.shape[1]
     seq_count = lengths.shape[0]
     block_start = lax.axis_index("mp") * block_width
-    local_in_w = lax.dynamic_slice_in_dim(proj_in_w, block_start, block_width, 0)
     local_out_w = lax.dynamic_slice_in_dim(proj_out_w, block_start, block_width, 0)
-    part_in = jnp.dot(attn_out, local_in_w, preferred_element_type=jnp.float32)
     part_out = jnp.dot(cotangent, local_out_w, preferred_element_type=jnp.float32)
-    proj_in, proj_out = lax.psum((part_in, part_out), "mp")
-    layer_out, grad_in = both_products(n, attn_out, cotangent, out_weight)
+    proj_out = lax.psum(part_out, "mp")
+    layer_out, grad_in, proj_in = both_products(n, attn_out, cotangent, out_weight, proj_in_w.T)
     slot_index = jnp.arange(tok_rows, dtype=jnp.int32)
     example_ids = slot_index // LEN
     offsets = slot_index % LEN
@@ -374,13 +384,17 @@
         proj_out.reshape(seq_count, LEN, rank_width),
         precision=HIGHEST_PRECISION,
     ).reshape(seq_count, rank_width * rank_width)
-    scores = lax.dot_general(
-        kronecker,
-        lax.all_gather(queries, "dp", axis=1, tiled=True).astype(jnp.float32),
+    high = lax.reduce_precision(kronecker, 8, 7)
+    middle = lax.reduce_precision(kronecker - high, 8, 7)
+    low = kronecker - high - middle
+    terms = jnp.concatenate([high, middle, low], axis=0).astype(jnp.bfloat16)
+    products = lax.dot_general(
+        terms,
+        lax.all_gather(queries, "dp", axis=1, tiled=True),
         (((1,), (1,)), ((), ())),
-        precision=HIGHEST_PRECISION,
         preferred_element_type=jnp.float32,
     )
+    scores = jnp.sum(products.reshape(3, seq_count, -1), axis=0)
     return (layer_out, grad_in, scores)
 
 

time: 249 us -> 243 us (0.976)
  matrix products: 9.78 us -> 6.07 us
  Pallas kernels: 216 us -> 213 us
    dot_general x2 -> x1, matrix products: 6.27 us -> 2.23 us  [per_device(): lax.dot_general(terms, lax.all_gather(queries, 'dp', axis=1, tiled=True),...]
    pallas_call x1, Pallas kernels: 216 us -> 213 us  [both_products(): pl.pallas_call(functools.partial(kernel, n, narrow), out_shape=(out, out,...]
  transfers between devices with their start and end apart: 2 -> 2, of which waited for: 0 -> 0; matrix products, arithmetic and copies ran while one was open for 1% -> 1% of each run, Pallas kernels for 87% -> 88%
where the time goes in v3:
time: 243 us
  Pallas kernels  213 us (88%)
  between operations  15.6 us (6%)
  matrix products  6.07 us (2%)
  local copies, waits for them, and re-layouts  5.63 us (2%)
    pallas_call x1, Pallas kernels, both_products(): pl.pallas_call(functools.partial(kernel, n, narrow), out_shape=(out, out,...  213 us
  transfers between devices with their start and end apart: 2, of which 0 were waited for; matrix products, arithmetic and copies ran while one was open for 1% of the time, Pallas kernels for 88%

profile of v3, /device:TPU:0, one launch (start us, length us, event | category | flops | bytes accessed | tf_op | source)
XLA Modules:
  0.0 242.9 jit_solution(9972036176669800887)
XLA Ops:
  8.0 0.0 copy-start
  8.0 0.0 all-reduce.2.cloned.1.call-start
  8.1 1.2 copy-done
  9.2 2.3 fusion
  11.6 0.7 copy.17
  12.2 0.0 all-reduce.2.cloned.1.call-update
  12.3 0.0 all-gather.2.cloned.1.call-start
  12.3 0.5 all-gather.2.cloned.1.call-update
  12.8 0.0 copy-start.3
  12.9 213.0 %shard_map.94 = (bf16[512,2048]{1,0:T(8,128)(2,1)}, bf16[512,2048]{1,0:T(8,128)(2,1)}, f32[512,64]{1,0:T(8,128)}) custom-call(bf16[512,2048]{1,0:T(8,128)(2,1)} %attn_hbm.1, bf16[512,2048]{1,0:T(8,128)(2,1)} %cot_hbm.1, bf16[8192,2048]{1,0:T(8,128)(2,1)} %w_hbm.1, bf16[64,8192]{1,0:T(8,128)(2,1)} %bitcast.14), custom_call_target="tpu_custom_call" | custom-call | flops 34359738368 | bytes 419430400 | tf_op jit(solution)/shard_map/pallas_call | solution.py:327
  225.9 0.0 copy-start.2
  225.9 0.0 copy-done.3
  225.9 0.1 fusion.9
  226.0 1.2 broadcast_multiply_fusion
  227.2 0.0 all-reduce.2.cloned.1.call-done
  227.3 1.5 fusion.19
  228.8 0.1 reshape.44
  228.9 0.0 all-gather.2.cloned.1.call-done
  228.9 2.2 fusion.2
  231.2 0.6 reduce_sum.19
  231.8 0.0 copy-done.2
  231.8 0.0 copy-start.1
  231.8 1.3 copy.21
  233.1 1.0 copy-done.1
  234.1 1.3 copy.22
  (3 shorter events, 0.1 us)
Async XLA Ops:
  8.0 1.2 copy-start
  8.0 219.2 %all-reduce.2.cloned.1.call-start = ((), (), s32[]{:S(2)}) async-start(), calls=%async_computation | async-start | bytes 262144 | tf_op jit(solution)/shard_map/psum | solution.py:370
  12.3 216.7 %all-gather.2.cloned.1.call-start = ((), (), s32[]{:S(2)}) async-start(), calls=%async_computation.1 | async-start | bytes 2621440 | tf_op jit(solution)/shard_map/all_gather | solution.py:393
  12.8 213.1 %copy-start.3 = (s32[2]{0:T(128)S(1)}, s32[2]{0:T(128)}, u32[]{:S(2)}) copy-start(s32[2]{0:T(128)} %param.13) | copy-start | bytes 28
  225.9 5.9 %copy-start.2 = (bf16[512,2048]{1,0:T(8,128)(2,1)S(1)}, bf16[512,2048]{1,0:T(8,128)(2,1)}, u32[]{:S(2)}) copy-start(bf16[512,2048]{1,0:T(8,128)(2,1)} %get-tuple-element.17) | copy-start | bytes 6291460
  231.8 2.3 copy-start.1
Sparse Core Ops, SparseCore 0:
  12.4 38.6 all-reduce.1
Sparse Core Ops, SparseCore 1:
  14.3 25.1 all-gather.1

commit v4 on v3

--- a/solution.py
+++ b/solution.py
@@ -205,13 +205,13 @@
         send_r = (late_r >= 0) & (d_r > me)
         send_l = (late_l >= 0) & (d_l < me)
 
-        @pl.when(send_r)
-        def _():
-            w_load(d_r, 0).start()
-
-        @pl.when(send_l)
-        def _():
-            w_load(d_l, 1).start()
+        @pl.when(ag_l)
+        def _():
+            w_load(from_left, 0).start()
+
+        @pl.when(ag_r)
+        def _():
+            w_load(from_right, 1).start()
 
         def pass_on(c, top):
             @pl.when(ag_l)
@@ -236,6 +236,24 @@
 
         lax.fori_loop(0, CHUNKS, pass_on, 0)
 
+        @pl.when(ag_l)
+        def _():
+            w_load(from_left, 0).wait()
+            forward(from_left, 0)
+
+        @pl.when(ag_r)
+        def _():
+            w_load(from_right, 1).wait()
+            forward(from_right, 1)
+
+        @pl.when(send_r)
+        def _():
+            w_load(d_r, 0).start()
+
+        @pl.when(send_l)
+        def _():
+            w_load(d_l, 1).start()
+
         @pl.when(send_r)
         def _():
             w_load(d_r, 0).wait()
@@ -256,24 +274,6 @@
             return top
 
         lax.fori_loop(0, CHUNKS, chunk, 0)
-
-        @pl.when(ag_l)
-        def _():
-            w_load(from_left, 0).start()
-
-        @pl.when(ag_r)
-        def _():
-            w_load(from_right, 1).start()
-
-        @pl.when(ag_l)
-        def _():
-            w_load(from_left, 0).wait()
-            forward(from_left, 0)
-
-        @pl.when(ag_r)
-        def _():
-            w_load(from_right, 1).wait()
-            forward(from_right, 1)
         return top
 
     own()

time: 243 us -> 227 us (0.934)
  Pallas kernels: 213 us -> 196 us
    pallas_call x1, Pallas kernels: 213 us -> 196 us  [both_products(): pl.pallas_call(functools.partial(kernel, n, narrow), out_shape=(out, out,...]
  transfers between devices with their start and end apart: 2 -> 2, of which waited for: 0 -> 0; matrix products, arithmetic and copies ran while one was open for 1% -> 1% of each run, Pallas kernels for 88% -> 87%
where the time goes in v4:
time: 227 us; the launch traced here: 226 us
  Pallas kernels  196 us (86%)
  between operations  15.6 us (7%)
  matrix products  6.07 us (3%)
  local copies, waits for them, and re-layouts  5.63 us (2%)
    pallas_call x1, Pallas kernels, both_products(): pl.pallas_call(functools.partial(kernel, n, narrow), out_shape=(out, out,...  196 us
    unnamed x10, local copies, waits for them, and re-layouts  4.85 us
  transfers between devices with their start and end apart: 2, of which 0 were waited for; matrix products, arithmetic and copies ran while one was open for 1% of the time, Pallas kernels for 87%

profile of v4, /device:TPU:0, one launch (start us, length us, event | category | flops | bytes accessed | tf_op | source)
XLA Modules:
  0.0 226.3 jit_solution(7656421723382391456)
XLA Ops:
  8.0 0.0 copy-start
  8.0 0.0 all-reduce.2.cloned.1.call-start
  8.1 1.2 copy-done
  9.2 2.3 %fusion = f32[64,512]{1,0:T(8,128)S(1)} fusion(bf16[512,2048]{1,0:T(8,128)(2,1)} %cot_hbm.1, bf16[8192,64]{0,1:T(8,128)(2,1)S(1)} %copy-done, s32[]{:T(128)S(6)} %select_n.25), kind=kOutput, calls=%fused_computation | convolution fusion | flops 134217728 | bytes 2490372 | tf_op jit(solution)/shard_map/dot_general | solution.py:369
  11.6 0.7 copy.17
  12.2 0.0 all-reduce.2.cloned.1.call-update
  12.3 0.0 all-gather.2.cloned.1.call-start
  12.3 0.5 all-gather.2.cloned.1.call-update
  12.8 0.0 copy-start.3
  12.9 196.4 %shard_map.94 = (bf16[512,2048]{1,0:T(8,128)(2,1)}, bf16[512,2048]{1,0:T(8,128)(2,1)}, f32[512,64]{1,0:T(8,128)}) custom-call(bf16[512,2048]{1,0:T(8,128)(2,1)} %attn_hbm.1, bf16[512,2048]{1,0:T(8,128)(2,1)} %cot_hbm.1, bf16[8192,2048]{1,0:T(8,128)(2,1)} %w_hbm.1, bf16[64,8192]{1,0:T(8,128)(2,1)} %bitcast.14), custom_call_target="tpu_custom_call" | custom-call | flops 34359738368 | bytes 419430400 | tf_op jit(solution)/shard_map/pallas_call | solution.py:327
  209.3 0.0 copy-start.2
  209.3 0.0 copy-done.3
  209.3 0.1 fusion.9
  209.4 1.2 broadcast_multiply_fusion
  210.6 0.0 all-reduce.2.cloned.1.call-done
  210.7 1.5 fusion.19
  212.2 0.1 reshape.44
  212.3 0.0 all-gather.2.cloned.1.call-done
  212.3 2.2 fusion.2
  214.6 0.6 reduce_sum.19
  215.2 0.0 copy-done.2
  215.2 0.0 copy-start.1
  215.2 1.3 copy.21
  216.5 1.0 copy-done.1
  217.6 1.3 copy.22
  (3 shorter events, 0.1 us)
Async XLA Ops:
  8.0 1.2 copy-start
  8.0 202.6 %all-reduce.2.cloned.1.call-start = ((), (), s32[]{:S(2)}) async-start(), calls=%async_computation | async-start | bytes 262144 | tf_op jit(solution)/shard_map/psum | solution.py:370
  12.3 200.1 %all-gather.2.cloned.1.call-start = ((), (), s32[]{:S(2)}) async-start(), calls=%async_computation.1 | async-start | bytes 2621440 | tf_op jit(solution)/shard_map/all_gather | solution.py:393
  12.8 196.5 %copy-start.3 = (s32[2]{0:T(128)S(1)}, s32[2]{0:T(128)}, u32[]{:S(2)}) copy-start(s32[2]{0:T(128)} %param.13) | copy-start | bytes 28
  209.3 5.9 %copy-start.2 = (bf16[512,2048]{1,0:T(8,128)(2,1)S(1)}, bf16[512,2048]{1,0:T(8,128)(2,1)}, u32[]{:S(2)}) copy-start(bf16[512,2048]{1,0:T(8,128)(2,1)} %get-tuple-element.17) | copy-start | bytes 6291460
  215.2 2.3 %copy-start.1 = (bf16[512,2048]{1,0:T(8,128)(2,1)S(1)}, bf16[512,2048]{1,0:T(8,128)(2,1)}, u32[]{:S(2)}) copy-start(bf16[512,2048]{1,0:T(8,128)(2,1)} %get-tuple-element.18) | copy-start | bytes 6291460
Sparse Core Ops, SparseCore 0:
  12.4 38.6 all-reduce.1
Sparse Core Ops, SparseCore 1:
  14.3 25.2 all-gather.1
